TPU v7x, 256 devices: a whole 4x4x8 slice. The times are simulated.
256 devices in a mesh: section: 8 (over z_hi, core), attn: 32 (over y, z_lo, x).
Axes of the slice: x: 4, y: 4, z: 8 (z_hi: 4, z_lo: 2; z = z_hi * 2 + z_lo), core: 2. Of those that a mesh axis runs over, the one named last changes fastest.
Arguments:
- queries: bfloat16 [8, 4096, 4096], P('section', 'attn'), may hold values from -150 to 150
- keys: bfloat16 [8, 4096, 512], P('section', 'attn'), may hold values from -6 to 6
- values: bfloat16 [8, 4096, 512], P('section', 'attn'), may hold values from -6 to 6
- handoff: bfloat16 [8, 4096, 8192], P('section', 'attn'), may hold values from -6 to 6
- doc_lengths: int32 [8, 8], P('section'), may hold values from 1 to 1024, 4096 in all within a row
- task_lengths: int32 [8, 32, 32], P('section'), may hold values from 1 to 8, 128 in all within a row
- assignment: int32 [8, 32, 32], P('section'), may hold values from 0 to 31, each once within a row
Outputs:
- context: bfloat16 [8, 4096, 4096], P('section', 'attn')
- task_lse: float32 [8, 8192, 32], P('section', 'attn')
- received: bfloat16 [8, 4096, 8192], P('section', 'attn')
Inputs may be any that keep to these rules, and one draw needn't show every extreme that they name: `doc_lengths`: documents follow one another along each section's sequence in the order given. `task_lengths`: row [s, j] cuts owner j's 128 tokens, in order, into 32 tasks. `assignment`: row [s, j] sends owner j's 32 tasks to 32 different workers.
All inputs are finite; a program needn't handle non-finite values.
Results may differ from a plain program's by a relative error of at most 0.0046.
Values may be sent and summed in bfloat16 or wider, within the bound.
A program may use at most 128 MiB of HBM per device.

v0:
```python
import jax
import jax.numpy as jnp
from jax import lax
from jax.sharding import PartitionSpec as P

HQ = 32
HK = 4
HD = 128
DOC_MAX = 1024


def from_behind(shard, axis, by):
    count = lax.axis_size(axis)
    pairs = [(i, i + by) for i in range(count) if 0 <= i + by < count]
    return lax.ppermute(shard, axis, pairs)


def doc_of(positions, lengths):
    ends = jnp.cumsum(lengths)
    found = jnp.sum((positions[..., None] >= ends).astype(jnp.int32), -1)
    return jnp.where(positions < 0, -1, found)


def attend(query_rows, query_pos, key_window, value_window, key_pos, lengths):
    group = HQ // HK
    count = query_rows.shape[0]
    width = key_window.shape[0]
    query_heads = query_rows.reshape(count, HK, group, HD)
    key_heads = key_window.reshape(width, HK, HD)
    value_heads = value_window.reshape(width, HK, HD)
    scores = jnp.einsum(
        "rhgd,khd->rhgk", query_heads, key_heads, preferred_element_type=jnp.float32
    ) * HD ** (-0.5)
    query_doc = doc_of(query_pos, lengths)
    key_doc = doc_of(key_pos, lengths)
    allowed = (
        (key_doc[None, :] == query_doc[:, None])
        & (key_pos[None, :] <= query_pos[:, None])
        & (key_pos[None, :] >= 0)
    )
    scores = jnp.where(allowed[:, None, None, :], scores, jnp.float32(-1e30))
    highest = jnp.max(scores, -1, keepdims=True)
    raised = jnp.exp(scores - highest)
    total = jnp.sum(raised, -1, keepdims=True)
    weights = (raised / total).astype(jnp.bfloat16)
    output = jnp.einsum("rhgk,khd->rhgd", weights, value_heads, preferred_element_type=jnp.float32)
    output = output.reshape(count, HQ * HD).astype(jnp.bfloat16)
    stats = (highest[..., 0] + jnp.log(total[..., 0])).reshape(count, HQ)
    filled = query_pos >= 0
    output = jnp.where(filled[:, None], output, jnp.zeros_like(output))
    stats = jnp.where(filled[:, None], stats, jnp.zeros_like(stats))
    return (output, stats)


def serve_sources(query_slots, position_slots, key_rows, value_rows, lengths, rows):
    sources = query_slots.shape[0]
    span = DOC_MAX + rows
    key_pad = jnp.concatenate(
        [jnp.zeros((DOC_MAX, key_rows.shape[1]), key_rows.dtype), key_rows], 0
    )
    value_pad = jnp.concatenate(
        [jnp.zeros((DOC_MAX, value_rows.shape[1]), value_rows.dtype), value_rows], 0
    )
    groups = 4
    within = sources // groups

    def one_source(query_rows, query_pos, source):
        first = source * rows
        key_window = lax.dynamic_slice_in_dim(key_pad, first, span, 0)
        value_window = lax.dynamic_slice_in_dim(value_pad, first, span, 0)
        key_pos = first - DOC_MAX + jnp.arange(span, dtype=jnp.int32)
        return attend(query_rows, query_pos, key_window, value_window, key_pos, lengths)

    outputs = []
    statistics = []
    for number in range(groups):
        low = number * within
        labels = low + jnp.arange(within, dtype=jnp.int32)
        output, stats = jax.vmap(one_source)(
            query_slots[low : low + within], position_slots[low : low + within], labels
        )
        outputs.append(output)
        statistics.append(stats)
    return (jnp.concatenate(outputs, 0), jnp.concatenate(statistics, 0))


def shards(queries, keys, values, handoff, doc_lengths, task_lengths, assignment):
    query_local = queries[0]
    key_local = keys[0]
    value_local = values[0]
    lengths = doc_lengths[0]
    owners = lax.axis_size("attn")
    myself = lax.axis_index("attn")
    rows = query_local.shape[0]
    capacity = 2 * rows // owners
    own_lengths = lax.dynamic_index_in_dim(task_lengths[0], myself, 0, keepdims=False)
    own_workers = lax.dynamic_index_in_dim(assignment[0], myself, 0, keepdims=False)
    task_ends = jnp.cumsum(own_lengths)
    task_starts = task_ends - own_lengths
    labels = jnp.arange(owners, dtype=jnp.int32)
    picked = own_workers[None, :] == labels[:, None]
    worker_start = jnp.sum(jnp.where(picked, task_starts[None, :], 0), 1)
    worker_length = jnp.sum(jnp.where(picked, own_lengths[None, :], 0), 1)
    slots = jnp.arange(capacity, dtype=jnp.int32)
    filled = slots[None, :] < worker_length[:, None]
    first_row = myself * rows
    send_pos = jnp.where(filled, first_row + worker_start[:, None] + slots[None, :], -1)
    tokens_here = jnp.arange(rows, dtype=jnp.int32)
    task_of = jnp.sum((tokens_here[:, None] >= task_ends[None, :]).astype(jnp.int32), 1)
    task_table = task_of[:, None] == labels[None, :]
    worker_of = jnp.sum(jnp.where(task_table, own_workers[None, :], 0), 1)
    rank_of = tokens_here - jnp.sum(jnp.where(task_table, task_starts[None, :], 0), 1)
    slot_of = worker_of * capacity + rank_of
    key_rows, value_rows = (
        lax.all_gather(key_local, "attn", axis=0, tiled=True),
        lax.all_gather(value_local, "attn", axis=0, tiled=True),
    )
    padded = jnp.concatenate(
        [query_local, jnp.zeros((capacity, query_local.shape[1]), query_local.dtype)], 0
    )
    taken = jax.vmap(lambda first: lax.dynamic_slice_in_dim(padded, first, capacity, 0))(
        worker_start
    )
    send_queries = jnp.where(filled[:, :, None], taken, jnp.zeros_like(taken))
    output, stats = serve_sources(
        lax.all_to_all(send_queries, "attn", split_axis=0, concat_axis=0, tiled=True),
        lax.all_to_all(send_pos, "attn", split_axis=0, concat_axis=0, tiled=True),
        key_rows,
        value_rows,
        lengths,
        rows,
    )
    returned = lax.all_to_all(output, "attn", split_axis=0, concat_axis=0, tiled=True)
    returned, stat_slots = (returned, stats)
    context = returned.reshape(owners * capacity, -1)[slot_of]
    task_stats = stat_slots.reshape(owners * capacity, -1)
    received = from_behind(handoff, "section", 1)
    return (context[None], task_stats[None], received)


def solution(mesh):
    in_specs = (
        P("section", "attn", None),
        P("section", "attn", None),
        P("section", "attn", None),
        P("section", "attn", None),
        P("section", None),
        P("section", None, None),
        P("section", None, None),
    )
    out_specs = (P("section", "attn", None), P("section", "attn", None), P("section", "attn", None))
    return jax.shard_map(shards, mesh=mesh, in_specs=in_specs, out_specs=out_specs, check_vma=False)
```

profile of v0, /device:TPU:192, one launch (start us, length us, event | category | flops | bytes accessed | tf_op | source)
XLA Modules:
  0.0 879.0 jit_solution(6140501026196726041)
XLA Ops:
  10.5 7.8 all-to-all-start
  21.1 37.0 %while.20 = (s32[]{:T(128)}, bf16[136,4096]{1,0:T(8,128)(2,1)S(1)}, s32[32,2]{0,1:T(2,128)S(1)}, bf16[32,8,4096]{2,1,0:T(8,128)(2,1)S(1)}) while((s32[]{:T(128)}, bf16[136,4096]{1,0:T(8,128)(2,1)S(1)}, s32[32,2]{0,1:T(2,128)S(1)}, bf16[32,8,4096]{2,1,0:T(8,128)(2,1)S(1)}) %tuple.169), condition=%wide.while_cond.2.clone, body=%wide.while_body.2.sunk.clone | while | flops 2 | bytes 131169 | solution.py:121
  61.0 8.3 all-to-all-start.1
  72.5 35.1 %all-to-all-done.1 = bf16[32,8,4096]{2,1,0:T(8,128)(2,1)S(1)} async-done(((bf16[32,8,4096]{2,1,0:T(8,128)(2,1)}), bf16[32,8,4096]{2,1,0:T(8,128)(2,1)S(1)}, u32[]{:S(2)}, u32[]{:S(2)}) %all-to-all-start.1) | async-done | bytes 2097184 | tf_op jit(solution)/shard_map/all_to_all | solution.py:126
  109.1 71.4 %all-gather.7.cloned.1.call-done = bf16[1,4096,512]{2,1,0:T(8,128)(2,1)} async-done(((bf16[1,128,512]{2,1,0:T(8,128)(2,1)}), bf16[1,4096,512]{2,1,0:T(8,128)(2,1)}) %all-gather.7.cloned.1.call-update) | async-done | bytes 4194320 | tf_op jit(solution)/shard_map/all_gather | solution.py:115
  180.6 4.9 concatenate.36
  185.5 4.5 broadcast.637.clone
  190.0 31.0 %while.26 = (s32[]{:T(128)}, bf16[5120,512]{1,0:T(8,128)(2,1)}, s32[8,2]{0,1:T(2,128)S(1)}, bf16[8,1152,512]{2,1,0:T(8,128)(2,1)}) while((s32[]{:T(128)}, bf16[5120,512]{1,0:T(8,128)(2,1)}, s32[8,2]{0,1:T(2,128)S(1)}, bf16[8,1152,512]{2,1,0:T(8,128)(2,1)}) %tuple.172), condition=%wide.while_cond.8.clone, body=%wide.while_body.8.sunk.clone | while | flops 2 | bytes 2359901 | solution.py:69
  221.0 14.0 %reshape.694 = bf16[8,1152,4,128]{3,2,1,0:T(4,128)(2,1)} reshape(bf16[8,1152,512]{2,1,0:T(8,128)(2,1)} %get-tuple-element.74) | data formatting | bytes 18874368 | tf_op jit(solution)/shard_map/vmap()/reshape | solution.py:29
  235.0 105.1 %all-gather.5.cloned.1.call-done = bf16[1,4096,512]{2,1,0:T(8,128)(2,1)} async-done(((bf16[1,128,512]{2,1,0:T(8,128)(2,1)}), bf16[1,4096,512]{2,1,0:T(8,128)(2,1)}) %all-gather.5.cloned.1.call-update) | async-done | bytes 4194320 | tf_op jit(solution)/shard_map/all_gather | solution.py:116
  340.1 4.8 concatenate.34
  344.9 4.5 broadcast.637.clone.1
  349.4 30.6 %while.25 = (s32[]{:T(128)}, bf16[5120,512]{1,0:T(8,128)(2,1)}, s32[8,2]{0,1:T(2,128)S(1)}, bf16[8,1152,512]{2,1,0:T(8,128)(2,1)}) while((s32[]{:T(128)}, bf16[5120,512]{1,0:T(8,128)(2,1)}, s32[8,2]{0,1:T(2,128)S(1)}, bf16[8,1152,512]{2,1,0:T(8,128)(2,1)}) %tuple.212), condition=%wide.while_cond.7.clone, body=%wide.while_body.7.sunk.clone | while | flops 2 | bytes 2359901 | solution.py:70
  380.1 14.0 %reshape.693 = bf16[8,1152,4,128]{3,2,1,0:T(4,128)(2,1)} reshape(bf16[8,1152,512]{2,1,0:T(8,128)(2,1)} %get-tuple-element.66) | data formatting | bytes 18874368 | tf_op jit(solution)/shard_map/vmap()/reshape | solution.py:30
  394.0 11.3 %fusion.23 = (f32[8,8,4,8]{3,1,2,0:T(8,128)S(1)}, f32[8,4,1152,8,8]{2,4,3,1,0:T(8,128)}) fusion(pred[8,8,1152]{2,1,0:T(8,128)(4,1)S(1)} %get-tuple-element.198, bf16[8,8,4,8,128]{4,3,2,1,0:T(8,128)(2,1)S(1)} %get-tuple-element.202, bf16[8,1152,4,128,1]{3,2,1,0,4:T(4,128)(2,1)} %bitcast.238), kind=kOutput, calls=%fused_computation.54 | convolution fusion | flops 611055616 | bytes 19480576 | tf_op jit(solution)/shard_map/vmap(rhgd,khd->rhgk)/dot_general | solution.py:31
  405.3 5.2 fusion.19
  411.8 7.5 fusion.56
  420.4 4.5 broadcast.637.clone.2
  424.9 31.6 %while.24 = (s32[]{:T(128)}, bf16[5120,512]{1,0:T(8,128)(2,1)}, s32[8,2]{0,1:T(2,128)S(1)}, bf16[8,1152,512]{2,1,0:T(8,128)(2,1)}) while((s32[]{:T(128)}, bf16[5120,512]{1,0:T(8,128)(2,1)}, s32[8,2]{0,1:T(2,128)S(1)}, bf16[8,1152,512]{2,1,0:T(8,128)(2,1)}) %tuple.202), condition=%wide.while_cond.6.clone, body=%wide.while_body.6.sunk.clone | while | flops 2 | bytes 2359901 | solution.py:69
  453.2 3.3 bitcast_dynamic-update-slice_fusion.33
  456.6 14.0 %reshape.691 = bf16[8,1152,4,128]{3,2,1,0:T(4,128)(2,1)} reshape(bf16[8,1152,512]{2,1,0:T(8,128)(2,1)} %get-tuple-element.58) | data formatting | bytes 18874368 | tf_op jit(solution)/shard_map/vmap()/reshape | solution.py:29
  470.6 4.5 broadcast.637.clone.3
  475.0 30.6 %while.23 = (s32[]{:T(128)}, bf16[5120,512]{1,0:T(8,128)(2,1)}, s32[8,2]{0,1:T(2,128)S(1)}, bf16[8,1152,512]{2,1,0:T(8,128)(2,1)}) while((s32[]{:T(128)}, bf16[5120,512]{1,0:T(8,128)(2,1)}, s32[8,2]{0,1:T(2,128)S(1)}, bf16[8,1152,512]{2,1,0:T(8,128)(2,1)}) %tuple.211), condition=%wide.while_cond.5.clone, body=%wide.while_body.5.sunk.clone | while | flops 2 | bytes 2359901 | solution.py:70
  505.7 14.0 %reshape.690 = bf16[8,1152,4,128]{3,2,1,0:T(4,128)(2,1)} reshape(bf16[8,1152,512]{2,1,0:T(8,128)(2,1)} %get-tuple-element.50) | data formatting | bytes 18874368 | tf_op jit(solution)/shard_map/vmap()/reshape | solution.py:30
  519.6 11.2 %fusion.22 = (f32[8,8,4,8]{3,1,2,0:T(8,128)S(1)}, f32[8,4,1152,8,8]{2,4,3,1,0:T(8,128)}) fusion(pred[8,8,1152]{2,1,0:T(8,128)(4,1)S(1)} %get-tuple-element.199, bf16[8,8,4,8,128]{4,3,2,1,0:T(8,128)(2,1)S(1)} %get-tuple-element.203, bf16[8,1152,4,128,1]{3,2,1,0,4:T(4,128)(2,1)} %bitcast.240), kind=kOutput, calls=%fused_computation.53 | convolution fusion | flops 611055616 | bytes 19480576 | tf_op jit(solution)/shard_map/vmap(rhgd,khd->rhgk)/dot_general | solution.py:31
  530.8 5.2 fusion.18
  537.3 7.0 fusion.59
  544.6 4.5 broadcast.637.clone.4
  549.1 31.6 %while.22 = (s32[]{:T(128)}, bf16[5120,512]{1,0:T(8,128)(2,1)}, s32[8,2]{0,1:T(2,128)S(1)}, bf16[8,1152,512]{2,1,0:T(8,128)(2,1)}) while((s32[]{:T(128)}, bf16[5120,512]{1,0:T(8,128)(2,1)}, s32[8,2]{0,1:T(2,128)S(1)}, bf16[8,1152,512]{2,1,0:T(8,128)(2,1)}) %tuple.203), condition=%wide.while_cond.4.clone, body=%wide.while_body.4.sunk.clone | while | flops 2 | bytes 2359901 | solution.py:69
  577.4 3.3 bitcast_dynamic-update-slice_fusion.31
  580.7 14.0 %reshape.688 = bf16[8,1152,4,128]{3,2,1,0:T(4,128)(2,1)} reshape(bf16[8,1152,512]{2,1,0:T(8,128)(2,1)} %get-tuple-element.42) | data formatting | bytes 18874368 | tf_op jit(solution)/shard_map/vmap()/reshape | solution.py:29
  594.7 4.5 broadcast.637.clone.5
  599.2 30.9 %while.21 = (s32[]{:T(128)}, bf16[5120,512]{1,0:T(8,128)(2,1)}, s32[8,2]{0,1:T(2,128)S(1)}, bf16[8,1152,512]{2,1,0:T(8,128)(2,1)}) while((s32[]{:T(128)}, bf16[5120,512]{1,0:T(8,128)(2,1)}, s32[8,2]{0,1:T(2,128)S(1)}, bf16[8,1152,512]{2,1,0:T(8,128)(2,1)}) %tuple.210), condition=%wide.while_cond.3.clone, body=%wide.while_body.3.sunk.clone | while | flops 2 | bytes 2359901 | solution.py:70
  630.1 14.1 %reshape.687 = bf16[8,1152,4,128]{3,2,1,0:T(4,128)(2,1)} reshape(bf16[8,1152,512]{2,1,0:T(8,128)(2,1)} %get-tuple-element.34) | data formatting | bytes 18874368 | tf_op jit(solution)/shard_map/vmap()/reshape | solution.py:30
  644.3 11.2 %fusion.21 = (f32[8,8,4,8]{3,1,2,0:T(8,128)S(1)}, f32[8,4,1152,8,8]{2,4,3,1,0:T(8,128)}) fusion(pred[8,8,1152]{2,1,0:T(8,128)(4,1)S(1)} %copy-done.15, bf16[8,8,4,8,128]{4,3,2,1,0:T(8,128)(2,1)S(1)} %get-tuple-element.204, bf16[8,1152,4,128,1]{3,2,1,0,4:T(4,128)(2,1)} %bitcast.241), kind=kOutput, calls=%fused_computation.52 | convolution fusion | flops 611055616 | bytes 19480576 | tf_op jit(solution)/shard_map/vmap(rhgd,khd->rhgk)/dot_general | solution.py:31
  655.5 5.2 fusion.17
  662.0 7.0 fusion.62
  669.3 4.5 broadcast.637.clone.6
  673.8 30.8 %while.19 = (s32[]{:T(128)}, bf16[5120,512]{1,0:T(8,128)(2,1)}, s32[8,2]{0,1:T(2,128)S(1)}, bf16[8,1152,512]{2,1,0:T(8,128)(2,1)}) while((s32[]{:T(128)}, bf16[5120,512]{1,0:T(8,128)(2,1)}, s32[8,2]{0,1:T(2,128)S(1)}, bf16[8,1152,512]{2,1,0:T(8,128)(2,1)}) %tuple.208), condition=%wide.while_cond.1.clone, body=%wide.while_body.1.sunk.clone | while | flops 2 | bytes 2359901 | solution.py:69
  704.5 14.0 %reshape.685 = bf16[8,1152,4,128]{3,2,1,0:T(4,128)(2,1)} reshape(bf16[8,1152,512]{2,1,0:T(8,128)(2,1)} %get-tuple-element.18) | data formatting | bytes 18874368 | tf_op jit(solution)/shard_map/vmap()/reshape | solution.py:29
  718.5 4.5 broadcast.637.clone.7
  723.1 30.7 %while.18 = (s32[]{:T(128)}, bf16[5120,512]{1,0:T(8,128)(2,1)}, s32[8,2]{0,1:T(2,128)S(1)}, bf16[8,1152,512]{2,1,0:T(8,128)(2,1)}) while((s32[]{:T(128)}, bf16[5120,512]{1,0:T(8,128)(2,1)}, s32[8,2]{0,1:T(2,128)S(1)}, bf16[8,1152,512]{2,1,0:T(8,128)(2,1)}) %tuple.209), condition=%wide.while_cond.clone, body=%wide.while_body.sunk.clone | while | flops 2 | bytes 2359901 | solution.py:70
  753.8 14.2 %reshape.682 = bf16[8,1152,4,128]{3,2,1,0:T(4,128)(2,1)} reshape(bf16[8,1152,512]{2,1,0:T(8,128)(2,1)} %get-tuple-element.10) | data formatting | bytes 18874368 | tf_op jit(solution)/shard_map/vmap()/reshape | solution.py:30
  768.0 11.2 %fusion.20 = (f32[8,8,4,8]{3,1,2,0:T(8,128)S(1)}, f32[8,4,1152,8,8]{2,4,3,1,0:T(8,128)}) fusion(pred[8,8,1152]{2,1,0:T(8,128)(4,1)S(1)} %copy-done.14, bf16[8,8,4,8,128]{4,3,2,1,0:T(8,128)(2,1)S(1)} %copy-done.13, bf16[8,1152,4,128,1]{3,2,1,0,4:T(4,128)(2,1)} %bitcast.239), kind=kOutput, calls=%fused_computation.51 | convolution fusion | flops 611055616 | bytes 19480576 | tf_op jit(solution)/shard_map/vmap(rhgd,khd->rhgk)/dot_general | solution.py:31
  779.3 5.2 fusion.16
  785.8 7.0 fusion.65
  795.3 6.7 all-to-all-start.2
  805.5 56.7 %collective-permute-done = bf16[1,128,8192]{2,1,0:T(8,128)(2,1)} collective-permute-done((bf16[1,128,8192]{2,1,0:T(8,128)(2,1)}, bf16[1,128,8192]{2,1,0:T(8,128)(2,1)}, u32[]{:S(2)}, u32[]{:S(2)}) %collective-permute-start) | collective-permute-done | bytes 2097184 | tf_op jit(solution)/shard_map/ppermute | solution.py:15
  (426 shorter events, 313.3 us)
Async XLA Ops:
  7.2 1.7 copy-start
  7.2 173.4 %all-gather.7.cloned.1.call-start = ((), (), s32[]{:S(2)}) async-start(), calls=%async_computation.4 | async-start | bytes 4325376 | tf_op jit(solution)/shard_map/all_gather | solution.py:115
  8.9 10.5 %copy-start.22 = (s32[32]{0:T(128)}, s32[32]{0:T(128)S(1)}, u32[]{:S(2)}) copy-start(s32[32]{0:T(128)S(1)} %reduce) | copy-start | bytes 388
  8.9 10.5 %copy-start.23 = (s32[32]{0:T(128)}, s32[32]{0:T(128)S(1)}, u32[]{:S(2)}) copy-start(s32[32]{0:T(128)S(1)} %dynamic-slice_bitcast_fusion) | copy-start | bytes 388
  9.6 0.9 copy-start.21
  10.5 50.5 %all-to-all-start = ((s32[32,1,8]{2,1,0:T(1,128)}), s32[32,1,8]{2,1,0:T(1,128)S(1)}, u32[]{:S(2)}, u32[]{:S(2)}) async-start(s32[32,1,8]{2,1,0:T(1,128)} %compare_select_fusion), calls=%async_computation | async-start | bytes 32768 | tf_op jit(solution)/shard_map/all_to_all | solution.py:127
  18.3 321.8 %all-gather.5.cloned.1.call-start = ((), (), s32[]{:S(2)}) async-start(), calls=%async_computation.3 | async-start | bytes 4325376 | tf_op jit(solution)/shard_map/all_gather | solution.py:116
  61.0 46.7 %all-to-all-start.1 = ((bf16[32,8,4096]{2,1,0:T(8,128)(2,1)}), bf16[32,8,4096]{2,1,0:T(8,128)(2,1)S(1)}, u32[]{:S(2)}, u32[]{:S(2)}) async-start(bf16[32,8,4096]{2,1,0:T(8,128)(2,1)} %broadcast_select_fusion), calls=%async_computation.1 | async-start | bytes 4194304 | tf_op jit(solution)/shard_map/all_to_all | solution.py:126
  405.3 14.0 %copy-start.7 = (f32[8,8,4,8]{3,1,2,0:T(8,128)}, f32[8,8,4,8]{3,1,2,0:T(8,128)S(1)}, u32[]{:S(2)}) copy-start(f32[8,8,4,8]{3,1,2,0:T(8,128)S(1)} %get-tuple-element.186) | copy-start | bytes 24580
  405.3 6.5 copy-start.4
  410.5 8.8 %copy-start.9 = (f32[8,8,4,8]{3,1,2,0:T(8,128)}, f32[8,8,4,8]{3,1,2,0:T(8,128)S(1)}, u32[]{:S(2)}) copy-start(f32[8,8,4,8]{3,1,2,0:T(8,128)S(1)} %fusion.19) | copy-start | bytes 24580
  530.8 6.4 copy-start.2
  630.1 14.1 %copy-start.15 = (pred[8,8,1152]{2,1,0:T(8,128)(4,1)S(1)}, pred[8,8,1152]{2,1,0:T(8,128)(4,1)}, u32[]{:S(2)}) copy-start(pred[8,8,1152]{2,1,0:T(8,128)(4,1)} %get-tuple-element.200) | copy-start | bytes 221188
  655.5 6.4 copy-start.5
  669.0 4.8 copy-start.16
  753.8 14.2 %copy-start.13 = (bf16[8,8,4,8,128]{4,3,2,1,0:T(8,128)(2,1)S(1)}, bf16[8,8,4,8,128]{4,3,2,1,0:T(8,128)(2,1)}, u32[]{:S(2)}) copy-start(bf16[8,8,4,8,128]{4,3,2,1,0:T(8,128)(2,1)} %get-tuple-element.205) | copy-start | bytes 1572868
  753.8 14.2 %copy-start.14 = (pred[8,8,1152]{2,1,0:T(8,128)(4,1)S(1)}, pred[8,8,1152]{2,1,0:T(8,128)(4,1)}, u32[]{:S(2)}) copy-start(pred[8,8,1152]{2,1,0:T(8,128)(4,1)} %get-tuple-element.201) | copy-start | bytes 221188
  779.3 6.5 copy-start.3
  784.5 8.3 copy-start.11
  785.8 7.5 copy-start.6
  785.8 7.5 copy-start.20
  785.8 7.6 copy-start.19
  785.8 7.7 copy-start.18
  785.8 7.8 copy-start.17
  792.9 69.4 %copy-start.8 = (f32[8,8,4,8]{3,1,2,0:T(8,128)S(1)}, f32[8,8,4,8]{3,1,2,0:T(8,128)}, u32[]{:S(2)}) copy-start(f32[8,8,4,8]{3,1,2,0:T(8,128)} %copy-done.7) | copy-start | bytes 24580
  792.9 69.4 %copy-start.10 = (f32[8,8,4,8]{3,1,2,0:T(8,128)S(1)}, f32[8,8,4,8]{3,1,2,0:T(8,128)}, u32[]{:S(2)}) copy-start(f32[8,8,4,8]{3,1,2,0:T(8,128)} %copy-done.9) | copy-start | bytes 24580
  793.2 69.6 %copy-start.12 = (f32[8,8,4,8]{3,1,2,0:T(8,128)S(1)}, f32[8,8,4,8]{3,1,2,0:T(8,128)}, u32[]{:S(2)}) copy-start(f32[8,8,4,8]{3,1,2,0:T(8,128)} %copy-done.11) | copy-start | bytes 24580
  795.3 71.4 %all-to-all-start.2 = ((bf16[32,8,4096]{2,1,0:T(8,128)(2,1)}), bf16[32,8,4096]{2,1,0:T(8,128)(2,1)S(1)}, u32[]{:S(2)}, u32[]{:S(2)}) async-start(bf16[32,8,4096]{2,1,0:T(8,128)(2,1)} %pad_maximum_fusion), calls=%async_computation.2 | async-start | bytes 4194304 | tf_op jit(solution)/shard_map/all_to_all | solution.py:133
  802.0 69.9 %copy-start.1 = (s32[1,32,32]{2,1,0:T(8,128)S(1)}, s32[1,32,32]{2,1,0:T(8,128)}, u32[]{:S(2)}) copy-start(s32[1,32,32]{2,1,0:T(8,128)} %param.13) | copy-start | bytes 12292
  802.1 60.2 %collective-permute-start = (bf16[1,128,8192]{2,1,0:T(8,128)(2,1)}, bf16[1,128,8192]{2,1,0:T(8,128)(2,1)}, u32[]{:S(2)}, u32[]{:S(2)}) collective-permute-start(bf16[1,128,8192]{2,1,0:T(8,128)(2,1)} %param.10), channel_id=1, source_target_pairs={{0,32},{32,64},{64,96},{96,128},{128,160},{160,192},{192,224},{1,3... | collective-permute-start | bytes 6291464 | tf_op jit(solution)/shard_map/ppermute | solution.py:15
Sparse Core Ops, SparseCore 0:
  9.8 170.7 all-gather.6
  182.4 157.7 all-gather.4
where the time goes:
time: 895 us; the launch traced here: 879 us
  local copies, waits for them, and re-layouts  460 us (51%)
  waiting for transfers between devices  270 us (30%)
  matrix products  73.4 us (8%)
  other arithmetic  35.5 us (4%)
  starting transfers between devices  24.8 us (3%)
  between operations  14.8 us (2%)
    gather x288, local copies, waits for them, and re-layouts  284 us
    all_gather x1, waiting for transfers between devices, shards(): lax.all_gather(value_local, 'attn', axis=0, tiled=True)  105 us
    all_gather x1, waiting for transfers between devices, shards(): lax.all_gather(key_local, 'attn', axis=0, tiled=True)  71.4 us
    ppermute x1, waiting for transfers between devices, from_behind(): return lax.ppermute(shard, axis, pairs)  56.7 us
    reshape x4, local copies, waits for them, and re-layouts, attend(): value_heads = value_window.reshape(width, HK, HD)  56.3 us
    reshape x4, local copies, waits for them, and re-layouts, attend(): key_heads = key_window.reshape(width, HK, HD)  56 us
    unnamed x59, local copies, waits for them, and re-layouts  45 us
    dot_general x4, matrix products, attend(): jnp.einsum('rhgd,khd->rhgk', query_heads, key_heads, preferred_element_ty...  44.9 us
  transfers between devices with their start and end apart: 6, of which 4 were waited for; matrix products, arithmetic and copies ran while one was open for 12% of the time, Pallas kernels for 0%

commit v1 on v0

v1 whole, which is shorter than its diff:
```python
import math

import jax
import jax.numpy as jnp
from jax import lax
from jax.experimental import pallas as pl
from jax.experimental.pallas import tpu as pltpu
from jax.sharding import PartitionSpec as P

MESH = pl.DeviceIdType.MESH
F32 = jnp.float32
BF16 = jnp.bfloat16
HQ = 32
HK = 4
HD = 128
GROUP = HQ // HK
ROWS = 128
WIDE = 8192
ROLES = 9
LONG = 3
PIECE = 16
SCALE = HD ** -0.5
EXP2 = SCALE / math.log(2.0)


def section_of(z, core):
    return (z // 2) * 2 + core


def owner_of(y, z, x):
    return y * 8 + (z % 2) * 4 + x


def long_pieces(z):
    return jnp.where((z == 1) | (z == 4), 3, jnp.where((z == 2) | (z == 3), 2, 0))


def kernel(
    q_hbm, k_hbm, v_hbm, h_hbm, dl_hbm, tl_hbm, as_hbm,
    ctx, lse, rec,
    qs, kb, vb, sc, mx, rl, stat, mid, ends, tl, ws,
    pack, t1, t2, t3,
    q_sem, own_sem, int_sem, kv_send, kv_recv, h_send, h_recv, m_send, m_recv,
    s_send, s_recv,
):
    s = lax.axis_index("section")
    a = lax.axis_index("attn")
    core = s % 2
    y = a // 8
    zl = (a // 4) % 2
    x = a % 4
    z = (s // 2) * 2 + zl
    up = (z + 3) % 8
    down = (z + 5) % 8
    right = a - x + (x + 1) % 4
    left = a - x + (x + 3) % 4

    sender = (core == 1) & (z < 6)
    own_long = jnp.where(core == 1, long_pieces(z), 0)
    mid_long = jnp.where(core == 0, long_pieces(up), 0)
    is_sender = own_long > 0
    is_mid = mid_long > 0
    last_long = jnp.where((core == 0) & (z >= 2), long_pieces((z + 6) % 8), 0)
    is_last = last_long > 0

    for h in range(HQ):
        pltpu.make_async_copy(
            q_hbm.at[0, :, pl.ds(h * HD, HD)], qs.at[h], q_sem.at[h]
        ).start()
    own = [
        pltpu.make_async_copy(k_hbm.at[0], kb.at[0], own_sem.at[0]),
        pltpu.make_async_copy(v_hbm.at[0], vb.at[0], own_sem.at[1]),
    ]
    ints = [
        pltpu.make_async_copy(dl_hbm, ends, int_sem.at[0]),
        pltpu.make_async_copy(tl_hbm.at[0], tl, int_sem.at[1]),
        pltpu.make_async_copy(as_hbm.at[0], ws, int_sem.at[2]),
    ]
    for copy in own + ints:
        copy.start()

    barrier = pltpu.get_barrier_semaphore()

    def greet(device):
        pl.semaphore_signal(barrier, inc=1, device_id=device, device_id_type=MESH)

    @pl.when(s > 0)
    def _():
        greet((s - 1, a))

    @pl.when(is_mid)
    def _():
        greet((section_of(up, 1), owner_of(y, up, x)))

    @pl.when(is_last)
    def _():
        greet((section_of(up, 0), owner_of(y, up, x)))

    @pl.when((zl == 1) | (y > 0))
    def _():
        greet((s, a - 4))

    @pl.when(zl == 0)
    def _():
        greet((s, a + 4))

    @pl.when((zl == 1) & (y == 0))
    def _():
        pass

    for d in range(1, 4):
        greet((s, a - x + (x + d) % 4))
        greet((s, (a + 8 * d) % 32))
    expected = 6 + jnp.where(s < 7, 1, 0) + jnp.where(is_sender, 1, 0) + jnp.where(is_mid, 1, 0)
    expected = expected + jnp.where((zl == 0) | (y < 3), 1, 0) + jnp.where(zl == 1, 1, 0)
    pl.semaphore_wait(barrier, expected)

    hbm = (k_hbm, v_hbm)
    buf = (kb, vb)

    def block(t, n, source, role, device):
        return pltpu.make_async_remote_copy(
            source, buf[t].at[role], kv_send.at[t, n], kv_recv.at[t, role],
            device_id=(s, device), device_id_type=MESH,
        )

    c_ok = (zl == 1) | (y > 0)
    odd = x % 2 == 1
    across = jnp.minimum(a + 4, 31)
    above = jnp.minimum(a + 8, 31)

    def transfers(t):
        return [
            (y < 3, block(t, 0, hbm[t].at[0], 1, above)),
            ((zl == 0) | (y < 3), block(t, 1, hbm[t].at[0], 2, across)),
            (x < 3, block(t, 2, hbm[t].at[0], 4, right)),
            (x == 0, block(t, 3, hbm[t].at[0], 3, left)),
            ((x == 3) & (y > 0), block(t, 4, buf[t].at[1], 4, right)),
            ((x > 0) & (y > 0), block(t, 5, buf[t].at[1], 3, left)),
            (c_ok, block(t, 6, buf[t].at[2], 6, right)),
            (c_ok, block(t, 7, buf[t].at[2], 5, left)),
            (odd & ((x == 3) | (y > 0)), block(t, 8, buf[t].at[3], 7, left)),
            ((x % 2 == 0) & ((x == 2) | (y > 0)), block(t, 9, buf[t].at[4], 7, right)),
            ((x % 2 == 0) & c_ok, block(t, 10, buf[t].at[5], 8, left)),
            (odd & c_ok, block(t, 11, buf[t].at[6], 8, right)),
        ]

    moves = (transfers(0), transfers(1))

    def send(t, *numbers):
        for n in numbers:
            cond, copy = moves[t][n]
            pl.when(cond)(copy.start)

    base = a - x

    def straight(other):
        return base + other - jnp.where(other > x, 8, 0)

    def crossed(other):
        return base - 4 + other

    xr, xl, xo = (x + 1) % 4, (x + 3) % 4, (x + 2) % 4
    owners = [
        a, a - 8, a - 4, straight(xr), straight(xl), crossed(xr), crossed(xl),
        straight(xo), crossed(xo),
    ]

    def arrive(t, role):
        @pl.when(owners[role] >= 0)
        def _():
            block(t, 0, hbm[t].at[0], role, a).wait_recv()

        @pl.when(owners[role] < 0)
        def _():
            buf[t][role] = jnp.zeros((ROWS, HK * HD), BF16)

    nxt = jnp.minimum(s + 1, 7)

    def direct(lo, rows, i):
        return pltpu.make_async_remote_copy(
            h_hbm.at[0, pl.ds(lo, rows)], rec.at[0, pl.ds(lo, rows)],
            h_send.at[i], h_recv.at[i], device_id=(nxt, a), device_id_type=MESH,
        )

    def piece(i):
        return direct(i * PIECE, PIECE, i)

    main = direct(LONG * PIECE, ROWS - LONG * PIECE, LONG)

    def leg1(i):
        return pltpu.make_async_remote_copy(
            h_hbm.at[0, pl.ds(i * PIECE, PIECE)], mid.at[pl.ds(i * PIECE, PIECE)],
            m_send.at[i], m_recv.at[i],
            device_id=(section_of(down, 0), owner_of(y, down, x)), device_id_type=MESH,
        )

    def leg2(i):
        return pltpu.make_async_remote_copy(
            mid.at[pl.ds(i * PIECE, PIECE)], rec.at[0, pl.ds(i * PIECE, PIECE)],
            m_send.at[LONG + i], h_recv.at[i],
            device_id=(section_of(down, 0), owner_of(y, down, x)), device_id_type=MESH,
        )

    def relay(i):
        @pl.when(mid_long > i)
        def _():
            leg1(i).wait_recv()
            leg2(i).start()

    send(0, 0, 1, 2, 3)
    send(1, 0, 1, 2, 3)
    for i in range(LONG):
        pl.when(own_long > i)(leg1(i).start)

    @pl.when(s < 7)
    def _():
        main.start()

    for i in range(LONG):
        pl.when((s < 7) & (own_long <= i))(piece(i).start)

    @pl.when(s == 0)
    def _():
        rec[...] = jnp.zeros_like(rec)

    for copy in ints + own:
        copy.wait()

    row = lax.broadcasted_iota(jnp.int32, (ROWS, ROWS), 0)
    lane = lax.broadcasted_iota(jnp.int32, (ROWS, ROWS), 1)
    position = a * ROWS + row
    first = jnp.zeros((ROWS, ROWS), jnp.int32)
    end = jnp.int32(0)
    for i in range(8):
        end = end + ends[0, i]
        first = jnp.where(position >= end, end, first)

    for h in range(HQ):
        pltpu.make_async_copy(
            q_hbm.at[0, :, pl.ds(h * HD, HD)], qs.at[h], q_sem.at[h]
        ).wait()

    def scores(role):
        key_pos = owners[role] * ROWS + lane
        bias = jnp.where((key_pos >= first) & (key_pos <= position), F32(0), F32(-1e30))

        def body(g, carry):
            keys = kb[role, :, pl.ds(pl.multiple_of(g * HD, HD), HD)]
            heads = pl.ds(g * GROUP, GROUP)
            found = lax.dot_general(
                qs[heads].reshape(GROUP * ROWS, HD), keys, (((1,), (1,)), ((), ())),
                preferred_element_type=F32,
            ).reshape(GROUP, ROWS, ROWS) + bias[None]
            sc[heads, :, role * ROWS:(role + 1) * ROWS] = found
            mx[heads] = found if role == 0 else jnp.maximum(mx[heads], found)
            return carry

        lax.fori_loop(0, HK, body, 0)

    scores(0)
    arrive(0, 1)
    send(0, 4, 5)
    arrive(0, 2)
    send(0, 6, 7)
    scores(1)
    arrive(1, 1)
    send(1, 4, 5)
    scores(2)
    arrive(1, 2)
    send(1, 6, 7)
    arrive(0, 3)
    arrive(0, 4)
    send(0, 8, 9)
    scores(3)
    scores(4)
    arrive(0, 5)
    arrive(0, 6)
    send(0, 10, 11)
    scores(5)
    scores(6)
    arrive(1, 3)
    arrive(1, 4)
    send(1, 8, 9)
    relay(0)
    arrive(1, 5)
    arrive(1, 6)
    send(1, 10, 11)
    arrive(0, 7)
    scores(7)
    arrive(0, 8)
    scores(8)
    relay(1)

    stat[...] = jnp.zeros_like(stat)

    def soft(h, carry):
        top = jnp.max(mx[h], axis=1, keepdims=True)
        raised = jnp.exp2((sc[h] - top) * F32(EXP2))
        total = jnp.sum(raised, axis=1, keepdims=True)
        sc[h] = raised
        rl[h] = jnp.broadcast_to(1.0 / total, (ROWS, ROWS))
        value = top * F32(SCALE) + jnp.log(total)
        stat[...] = jnp.where(lane == h, value, stat[...])
        return carry

    lax.fori_loop(0, HQ, soft, 0)
    relay(2)

    slots = lax.broadcasted_iota(jnp.int32, (256, 32), 0)
    tasks = lax.broadcasted_iota(jnp.int32, (256, 32), 1)
    lengths = tl[pl.ds(a, 1), :]
    workers = ws[pl.ds(a, 1), :]
    picked = workers == slots // 8
    which = jnp.sum(jnp.where(picked, tasks, 0), axis=1, keepdims=True)
    length = jnp.sum(jnp.where(picked, lengths, 0), axis=1, keepdims=True)
    start = jnp.sum(jnp.where(tasks < which, lengths, 0), axis=1, keepdims=True)
    rank = lax.broadcasted_iota(jnp.int32, (256, ROWS), 0) % 8
    token = lax.broadcasted_iota(jnp.int32, (256, ROWS), 1)
    table = jnp.where((token == start + rank) & (rank < length), F32(1), F32(0))
    packed = jnp.zeros((64, ROWS), F32)
    for i in range(4):
        moved = stat[...] if i == 0 else pltpu.roll(stat[...], 32 * i, 1)
        packed = packed + lax.dot_general(
            table[i * 64:(i + 1) * 64], moved, (((1,), (0,)), ((), ())),
            precision=lax.Precision.HIGHEST, preferred_element_type=F32,
        )
    pack[...] = packed.reshape(2, 4, 8, ROWS)

    other_z = jnp.where(zl == 0, a + 4, a - 4)
    stage1 = pltpu.make_async_remote_copy(
        pack.at[1 - zl], t1.at[zl], s_send.at[0], s_recv.at[0],
        device_id=(s, other_z), device_id_type=MESH,
    )
    stage1.start()
    t1[pl.ds(zl, 1)] = pack[pl.ds(zl, 1)]

    for role in (7, 8):
        arrive(1, role)

    def weighted(h, carry):
        weights = (sc[h] * jnp.tile(rl[h], (1, ROLES))).astype(BF16)
        lanes = pl.ds(pl.multiple_of((h // GROUP) * HD, HD), HD)
        rows = vb[:, :, lanes].reshape(ROLES * ROWS, HD)
        out = lax.dot_general(
            weights, rows, (((1,), (0,)), ((), ())), preferred_element_type=F32
        )
        ctx[0, :, pl.ds(pl.multiple_of(h * HD, HD), HD)] = out.astype(BF16)
        return carry

    lax.fori_loop(0, 8, weighted, 0)

    stage1.wait()
    stage2 = [
        pltpu.make_async_remote_copy(
            t1.at[:, (x + d) % 4], t2.at[x], s_send.at[d], s_recv.at[d],
            device_id=(s, base + (x + d) % 4), device_id_type=MESH,
        )
        for d in range(1, 4)
    ]
    for copy in stage2:
        copy.start()
    t2[pl.ds(x, 1)] = t1[:, pl.ds(x, 1)].reshape(1, 2, 8, ROWS)
    lax.fori_loop(8, 16, weighted, 0)
    for copy in stage2:
        copy.wait()
    stage3 = [
        pltpu.make_async_remote_copy(
            t2, t3.at[y], s_send.at[3 + d], s_recv.at[3 + d],
            device_id=(s, (a + 8 * d) % 32), device_id_type=MESH,
        )
        for d in range(1, 4)
    ]
    for copy in stage3:
        copy.start()
    t3[pl.ds(y, 1)] = t2[...].reshape(1, 4, 2, 8, ROWS)
    lax.fori_loop(16, HQ, weighted, 0)
    for copy in stage3:
        copy.wait()
    for from_y in range(4):
        for from_z in range(2):
            for from_x in range(4):
                tile = t3[from_y, from_x, from_z]
                mine = tile[:, 0:32]
                for i in range(1, 4):
                    mine = jnp.where(y == i, tile[:, 32 * i:32 * (i + 1)], mine)
                owner = from_y * 8 + from_z * 4 + from_x
                lse[0, owner * 8:(owner + 1) * 8, :] = mine

    for t in range(2):
        for cond, copy in moves[t]:
            pl.when(cond)(copy.wait_send)
    for i in range(LONG):
        pl.when(own_long > i)(leg1(i).wait_send)
        pl.when(mid_long > i)(leg2(i).wait_send)
        pl.when((s < 7) & (own_long <= i))(piece(i).wait_send)

    @pl.when(s < 7)
    def _():
        main.wait_send()

    @pl.when(s > 0)
    def _():
        for i in range(LONG):
            piece(i).wait_recv()
        main.wait_recv()


def shards(queries, keys, values, handoff, doc_lengths, task_lengths, assignment):
    anywhere = pl.BlockSpec(memory_space=pltpu.HBM)
    local = pl.BlockSpec(memory_space=pltpu.VMEM)
    dma = pltpu.SemaphoreType.DMA
    return pl.pallas_call(
        kernel,
        out_shape=(
            pltpu.VMEM((1, ROWS, HQ * HD), BF16),
            pltpu.VMEM((1, 256, HQ), F32),
            pltpu.VMEM((1, ROWS, WIDE), BF16),
        ),
        in_specs=[anywhere] * 7,
        out_specs=(local, local, local),
        scratch_shapes=[
            pltpu.VMEM((HQ, ROWS, HD), BF16),
            pltpu.VMEM((ROLES, ROWS, HK * HD), BF16),
            pltpu.VMEM((ROLES, ROWS, HK * HD), BF16),
            pltpu.VMEM((HQ, ROWS, ROLES * ROWS), F32),
            pltpu.VMEM((HQ, ROWS, ROWS), F32),
            pltpu.VMEM((HQ, ROWS, ROWS), F32),
            pltpu.VMEM((ROWS, ROWS), F32),
            pltpu.VMEM((LONG * PIECE, WIDE), BF16),
            pltpu.SMEM((1, 8), jnp.int32),
            pltpu.VMEM((32, 32), jnp.int32),
            pltpu.VMEM((32, 32), jnp.int32),
            pltpu.VMEM((2, 4, 8, ROWS), F32),
            pltpu.VMEM((2, 4, 8, ROWS), F32),
            pltpu.VMEM((4, 2, 8, ROWS), F32),
            pltpu.VMEM((4, 4, 2, 8, ROWS), F32),
            dma((HQ,)),
            dma((2,)),
            dma((3,)),
            dma((2, 12)),
            dma((2, ROLES)),
            dma((LONG + 1,)),
            dma((LONG + 1,)),
            dma((2 * LONG,)),
            dma((LONG,)),
            dma((7,)),
            dma((7,)),
        ],
        compiler_params=pltpu.CompilerParams(
            collective_id=0, has_side_effects=True, vmem_limit_bytes=52 << 20
        ),
    )(queries, keys, values, handoff, doc_lengths, task_lengths, assignment)


def solution(mesh):
    rows = P("section", "attn", None)
    small = P("section", None, None)
    return jax.shard_map(
        shards,
        mesh=mesh,
        in_specs=(rows, rows, rows, rows, P("section", None), small, small),
        out_specs=(rows, rows, rows),
        check_vma=False,
    )
```

time: 895 us -> 67.1 us (0.07); the launches traced: 879 us -> 67 us
  local copies, waits for them, and re-layouts: 460 us -> 2.98 us
  waiting for transfers between devices: 270 us -> 0 us
  matrix products: 73.4 us -> 0 us
  Pallas kernels: 0 us -> 63.4 us
  other arithmetic: 35.5 us -> 0 us
  starting transfers between devices: 24.8 us -> 0 us
  between operations: 14.8 us -> 0.64 us
    gather x289 -> x0, local copies, waits for them, and re-layouts: 286 us -> none
    all_gather x2 -> x0, waiting for transfers between devices: 177 us -> none  [the longest x1 105 us: shards(): lax.all_gather(value_local, 'attn', axis=0, tiled=True)]
    reshape x10 -> x0, local copies, waits for them, and re-layouts: 114 us -> none  [the longest x4 56.3 us: attend(): value_heads = value_window.reshape(width, HK, HD)]
    dot_general x8 -> x0, matrix products: 73.4 us -> none  [the longest x4 44.9 us: attend(): jnp.einsum('rhgd,khd->rhgk', query_heads, key_heads, preferred_element_ty...]
    pallas_call x0 -> x1, Pallas kernels: none -> 63.4 us  [shards(): pl.pallas_call(kernel, out_shape=(pltpu.VMEM((1, ROWS, HQ * HD), BF16), p...]
    ppermute x1 -> x0, waiting for transfers between devices: 56.7 us -> none  [from_behind(): return lax.ppermute(shard, axis, pairs)]
    unnamed x59 -> x2, local copies, waits for them, and re-layouts: 45 us -> 2.29 us
    all_to_all x3 -> x0, waiting for transfers between devices: 35.1 us -> none  [the longest x1 35.1 us: shards(): lax.all_to_all(send_queries, 'attn', split_axis=0, concat_axis=0, tiled=T...]
  transfers between devices with their start and end apart: 6 -> 0, of which waited for: 4 -> 0; matrix products, arithmetic and copies ran while one was open for 12% -> 0% of each run, Pallas kernels for 0% -> 0%
where the time goes in v1:
time: 67.1 us; the launch traced here: 67 us
  Pallas kernels  63.4 us (94%)
  local copies, waits for them, and re-layouts  2.98 us (4%)
    pallas_call x1, Pallas kernels, shards(): pl.pallas_call(kernel, out_shape=(pltpu.VMEM((1, ROWS, HQ * HD), BF16), p...  63.4 us
    unnamed x2, local copies, waits for them, and re-layouts  2.29 us

profile of v1, /device:TPU:192, one launch (start us, length us, event | category | flops | bytes accessed | tf_op | source)
XLA Modules:
  0.0 67.0 jit_solution(16371163563419622461)
XLA Ops:
  0.6 63.4 %shard_map.94 = (bf16[1,128,4096]{2,1,0:T(8,128)(2,1)S(1)}, f32[1,256,32]{2,1,0:T(8,128)S(1)}, bf16[1,128,8192]{2,1,0:T(8,128)(2,1)S(1)}) custom-call(bf16[1,128,4096]{2,1,0:T(8,128)(2,1)} %q_hbm.1, bf16[1,128,512]{2,1,0:T(8,128)(2,1)} %k_hbm.1, bf16[1,128,512]{2,1,0:T(8,128)(2,1)} %v_hbm.1, bf16[1,128,8192]{2,1,0:T(8,128)(2,1)} %h_hbm.1, s32[1,8]{1,0:T(1,128)} %dl_hbm.1, ...), custom_call_target="tpu_custom_call" | custom-call | tf_op jit(solution)/shard_map/pallas_call | solution.py:413
  64.0 1.0 %copy.13 = bf16[1,128,4096]{2,1,0:T(8,128)(2,1)} copy(bf16[1,128,4096]{2,1,0:T(8,128)(2,1)S(1)} %get-tuple-element.6) | data formatting | bytes 2097152
  65.0 0.7 %copy.10 = f32[1,256,32]{1,2,0:T(8,128)} copy(f32[1,256,32]{2,1,0:T(8,128)S(1)} %get-tuple-element.4) | data formatting | bytes 65536 | tf_op jit(solution)/shard_map/pallas_call | solution.py:413
  65.7 1.3 %copy.14 = bf16[1,128,8192]{2,1,0:T(8,128)(2,1)} copy(bf16[1,128,8192]{2,1,0:T(8,128)(2,1)S(1)} %get-tuple-element.8) | data formatting | bytes 4194304

commit v2 on v1

v2 whole, which is shorter than its diff:
```python
import math

import jax
import jax.numpy as jnp
from jax import lax
from jax.experimental import pallas as pl
from jax.experimental.pallas import tpu as pltpu
from jax.sharding import PartitionSpec as P

MESH = pl.DeviceIdType.MESH
F32 = jnp.float32
BF16 = jnp.bfloat16
HQ = 32
HK = 4
HD = 128
GROUP = HQ // HK
ROWS = 128
WIDE = 8192
ROLES = 9
LONG = 6
PIECE = 16
HALF = WIDE // 2
NEAR = 7
TAIL = 16
SCALE = HD ** -0.5
EXP2 = SCALE / math.log(2.0)


def section_of(z, core):
    return (z // 2) * 2 + core


def owner_of(y, z, x):
    return y * 8 + (z % 2) * 4 + x


def long_pieces(z):
    return jnp.where((z == 1) | (z == 4), 5, jnp.where((z == 2) | (z == 3), 3, 0))


def kernel(
    q_hbm, k_hbm, v_hbm, h_hbm, dl_hbm, tl_hbm, as_hbm,
    ctx, lse, rec,
    qs, kb, vb, sc, mx, mx2, top1, sum1, rl, rl2, stat, table, mid, ends, tl, ws,
    pack, t2, t3, turned,
    q_sem, own_sem, int_sem, kv_send, kv_recv, h_send, h_recv, m_send, m_recv,
    s_send, s_recv,
):
    s = lax.axis_index("section")
    a = lax.axis_index("attn")
    core = s % 2
    y = a // 8
    zl = (a // 4) % 2
    x = a % 4
    z = (s // 2) * 2 + zl
    up = (z + 3) % 8
    down = (z + 5) % 8
    right = a - x + (x + 1) % 4
    left = a - x + (x + 3) % 4

    sender = (core == 1) & (z < 6)
    own_long = jnp.where(core == 1, long_pieces(z), 0)
    mid_long = jnp.where(core == 0, long_pieces(up), 0)
    is_sender = own_long > 0
    is_mid = mid_long > 0
    last_long = jnp.where((core == 0) & (z >= 2), long_pieces((z + 6) % 8), 0)
    is_last = last_long > 0

    for h in range(HQ):
        pltpu.make_async_copy(
            q_hbm.at[0, :, pl.ds(h * HD, HD)], qs.at[h], q_sem.at[h]
        ).start()
    own = [
        pltpu.make_async_copy(k_hbm.at[0], kb.at[0], own_sem.at[0]),
        pltpu.make_async_copy(v_hbm.at[0], vb.at[0], own_sem.at[1]),
    ]
    ints = [
        pltpu.make_async_copy(dl_hbm, ends, int_sem.at[0]),
        pltpu.make_async_copy(tl_hbm.at[0], tl, int_sem.at[1]),
        pltpu.make_async_copy(as_hbm.at[0], ws, int_sem.at[2]),
    ]
    for copy in own + ints:
        copy.start()

    barrier = pltpu.get_barrier_semaphore()

    def greet(device):
        pl.semaphore_signal(barrier, inc=1, device_id=device, device_id_type=MESH)

    @pl.when(s > 0)
    def _():
        greet((s - 1, a))

    @pl.when(is_mid)
    def _():
        greet((section_of(up, 1), owner_of(y, up, x)))

    @pl.when(is_last)
    def _():
        greet((section_of(up, 0), owner_of(y, up, x)))

    @pl.when((zl == 0) & (y > 0))
    def _():
        greet((s, a - 4))

    plane = a - a % 8
    spot = a % 8
    for d in range(1, 8):
        greet((s, plane + (spot + d) % 8))
    for d in range(1, 4):
        greet((s, (a + 8 * d) % 32))
    expected = 10 + jnp.where(s < 7, 1, 0) + jnp.where(is_sender, 1, 0) + jnp.where(is_mid, 1, 0)
    expected = expected + jnp.where((zl == 1) & (y < 3), 1, 0)
    pl.semaphore_wait(barrier, expected)

    hbm = (k_hbm, v_hbm)
    buf = (kb, vb)

    def block(t, n, source, role, device):
        return pltpu.make_async_remote_copy(
            source, buf[t].at[role], kv_send.at[t, n], kv_recv.at[t, role],
            device_id=(s, device), device_id_type=MESH,
        )

    c_ok = (zl == 1) | (y > 0)
    odd = x % 2 == 1
    across = jnp.minimum(a + 4, 31)
    above = jnp.minimum(a + 8, 31)

    def transfers(t):
        return [
            (y < 3, block(t, 0, hbm[t].at[0], 1, above)),
            ((zl == 0) | (y < 3), block(t, 1, hbm[t].at[0], 2, across)),
            (x < 3, block(t, 2, hbm[t].at[0], 4, right)),
            (x == 0, block(t, 3, hbm[t].at[0], 3, left)),
            ((x == 3) & (y > 0), block(t, 4, buf[t].at[1], 4, right)),
            ((x > 0) & (y > 0), block(t, 5, buf[t].at[1], 3, left)),
            (c_ok, block(t, 6, buf[t].at[2], 6, right)),
            (c_ok, block(t, 7, buf[t].at[2], 5, left)),
            (odd & ((x == 3) | (y > 0)), block(t, 8, buf[t].at[3], 7, left)),
            ((x % 2 == 0) & ((x == 2) | (y > 0)), block(t, 9, buf[t].at[4], 7, right)),
            ((x % 2 == 0) & c_ok, block(t, 10, buf[t].at[5], 8, left)),
            (odd & c_ok, block(t, 11, buf[t].at[6], 8, right)),
        ]

    moves = (transfers(0), transfers(1))

    def send(t, *numbers):
        for n in numbers:
            cond, copy = moves[t][n]
            pl.when(cond)(copy.start)

    base = a - x

    def straight(other):
        return base + other - jnp.where(other > x, 8, 0)

    def crossed(other):
        return base - 4 + other

    xr, xl, xo = (x + 1) % 4, (x + 3) % 4, (x + 2) % 4
    owners = [
        a, a - 8, a - 4, straight(xr), straight(xl), crossed(xr), crossed(xl),
        straight(xo), crossed(xo),
    ]

    def arrive(t, role):
        @pl.when(owners[role] >= 0)
        def _():
            block(t, 0, hbm[t].at[0], role, a).wait_recv()

        @pl.when(owners[role] < 0)
        def _():
            buf[t][role] = jnp.zeros((ROWS, HK * HD), BF16)

    nxt = jnp.minimum(s + 1, 7)

    def direct(lo, rows, i):
        return pltpu.make_async_remote_copy(
            h_hbm.at[0, pl.ds(lo, rows)], rec.at[0, pl.ds(lo, rows)],
            h_send.at[i], h_recv.at[i], device_id=(nxt, a), device_id_type=MESH,
        )

    def part(i):
        return pl.ds((i // 2) * PIECE, PIECE), pl.ds((i % 2) * HALF, HALF)

    def piece(i):
        rows, lanes = part(i)
        return pltpu.make_async_remote_copy(
            h_hbm.at[0, rows, lanes], rec.at[0, rows, lanes],
            h_send.at[i], h_recv.at[i], device_id=(nxt, a), device_id_type=MESH,
        )

    late = ROWS - TAIL
    main = direct(LONG // 2 * PIECE, late - LONG // 2 * PIECE, LONG)
    rest = direct(late, TAIL, LONG + 1)
    held_back = (core == 1) & (zl == 0) & (s < 7)

    def leg1(i):
        rows, lanes = part(i)
        return pltpu.make_async_remote_copy(
            h_hbm.at[0, rows, lanes], mid.at[rows, lanes], m_send.at[i], m_recv.at[i],
            device_id=(section_of(down, 0), owner_of(y, down, x)), device_id_type=MESH,
        )

    def leg2(i):
        rows, lanes = part(i)
        return pltpu.make_async_remote_copy(
            mid.at[rows, lanes], rec.at[0, rows, lanes], m_send.at[LONG + i], h_recv.at[i],
            device_id=(section_of(down, 0), owner_of(y, down, x)), device_id_type=MESH,
        )

    def relay(i):
        @pl.when(mid_long > i)
        def _():
            leg1(i).wait_recv()
            leg2(i).start()

    send(0, 1, 0, 2, 3)
    send(1, 0, 2, 3)
    for i in range(2):
        pl.when(own_long > i)(leg1(i).start)
    send(1, 1)
    for i in range(2, LONG):
        pl.when(own_long > i)(leg1(i).start)

    @pl.when(s < 7)
    def _():
        main.start()

    for i in range(LONG):
        pl.when((s < 7) & (own_long <= i))(piece(i).start)
    pl.when((s < 7) & jnp.logical_not(held_back))(rest.start)

    @pl.when(s == 0)
    def _():
        rec[...] = jnp.zeros_like(rec)

    for copy in ints + own:
        copy.wait()

    row = lax.broadcasted_iota(jnp.int32, (ROWS, ROWS), 0)
    lane = lax.broadcasted_iota(jnp.int32, (ROWS, ROWS), 1)
    position = a * ROWS + row
    first = jnp.zeros((ROWS, ROWS), jnp.int32)
    end = jnp.int32(0)
    for i in range(8):
        end = end + ends[0, i]
        first = jnp.where(position >= end, end, first)

    for h in range(HQ):
        pltpu.make_async_copy(
            q_hbm.at[0, :, pl.ds(h * HD, HD)], qs.at[h], q_sem.at[h]
        ).wait()

    def scores(role, count, highest, fresh):
        bias = jnp.concatenate(
            [
                jnp.where(
                    (owners[r] * ROWS + lane >= first) & (owners[r] * ROWS + lane <= position),
                    F32(0), F32(-1e30),
                )
                for r in range(role, role + count)
            ],
            axis=1,
        )

        def body(g, carry):
            keys = kb[role:role + count, :, pl.ds(pl.multiple_of(g * HD, HD), HD)]
            heads = pl.ds(g * GROUP, GROUP)
            found = lax.dot_general(
                qs[heads].reshape(GROUP * ROWS, HD), keys.reshape(count * ROWS, HD),
                (((1,), (1,)), ((), ())), preferred_element_type=F32,
            ).reshape(GROUP, ROWS, count * ROWS) + bias[None]
            sc[heads, :, role * ROWS:(role + count) * ROWS] = found
            best = found[:, :, :ROWS]
            if count == 2:
                best = jnp.maximum(best, found[:, :, ROWS:])
            highest[heads] = best if fresh else jnp.maximum(highest[heads], best)
            return carry

        lax.fori_loop(0, HK, body, 0)

    near = NEAR * ROWS

    def soft_near(h, carry):
        top = jnp.max(mx[h], axis=1, keepdims=True)
        raised = jnp.exp2((sc[h, :, :near] - top) * F32(EXP2))
        sc[h, :, :near] = raised
        top1[h] = jnp.broadcast_to(top, (ROWS, ROWS))
        sum1[h] = jnp.broadcast_to(jnp.sum(raised, axis=1, keepdims=True), (ROWS, ROWS))
        return carry

    def soft_far(h, carry):
        top = jnp.max(mx2[h], axis=1, keepdims=True)
        raised = jnp.exp2((sc[h, :, near:] - top) * F32(EXP2))
        sc[h, :, near:] = raised
        total = jnp.sum(raised, axis=1, keepdims=True)
        before = top1[h]
        highest = jnp.maximum(before, top)
        lift1 = jnp.exp2((before - highest) * F32(EXP2))
        lift2 = jnp.exp2((top - highest) * F32(EXP2))
        total = sum1[h] * lift1 + total * lift2
        share = 1.0 / total
        rl[h] = lift1 * share
        rl2[h] = lift2 * share
        value = highest * F32(SCALE) + jnp.log(total)
        stat[...] = jnp.where(lane == h, value, stat[...])
        return carry

    def weighted(h, carry):
        factor = jnp.concatenate(
            [jnp.tile(rl[h], (1, NEAR)), jnp.tile(rl2[h], (1, ROLES - NEAR))], axis=1
        )
        weights = (sc[h] * factor).astype(BF16)
        lanes = pl.ds(pl.multiple_of((h // GROUP) * HD, HD), HD)
        rows = vb[:, :, lanes].reshape(ROLES * ROWS, HD)
        out = lax.dot_general(
            weights, rows, (((1,), (0,)), ((), ())), preferred_element_type=F32
        )
        ctx[0, :, pl.ds(pl.multiple_of(h * HD, HD), HD)] = out.astype(BF16)
        return carry

    def loop(body, low, high):
        lax.fori_loop(low, high, body, 0, unroll=2)

    scores(0, 1, mx, True)
    arrive(0, 1)
    send(0, 4, 5)
    arrive(0, 2)
    send(0, 6, 7)

    slots = lax.broadcasted_iota(jnp.int32, (256, 32), 0)
    tasks = lax.broadcasted_iota(jnp.int32, (256, 32), 1)
    lengths = tl[pl.ds(a, 1), :]
    workers = ws[pl.ds(a, 1), :]
    picked = workers == slots // 8
    which = jnp.sum(jnp.where(picked, tasks, 0), axis=1, keepdims=True)
    length = jnp.sum(jnp.where(picked, lengths, 0), axis=1, keepdims=True)
    start = jnp.sum(jnp.where(tasks < which, lengths, 0), axis=1, keepdims=True)
    rank = lax.broadcasted_iota(jnp.int32, (256, ROWS), 0) % 8
    token = lax.broadcasted_iota(jnp.int32, (256, ROWS), 1)
    table[...] = jnp.where((token == start + rank) & (rank < length), F32(1), F32(0))
    stat[...] = jnp.zeros_like(stat)

    scores(1, 2, mx, False)
    relay(0)
    arrive(0, 3)
    arrive(0, 4)
    send(0, 8, 9)
    arrive(1, 1)
    send(1, 4, 5)
    scores(3, 2, mx, False)
    relay(1)
    arrive(0, 5)
    arrive(0, 6)
    send(0, 10, 11)
    arrive(1, 2)
    send(1, 6, 7)
    scores(5, 2, mx, False)
    loop(soft_near, 0, 16)
    relay(2)
    arrive(1, 3)
    arrive(1, 4)
    send(1, 8, 9)
    loop(soft_near, 16, HQ)
    arrive(0, 7)
    arrive(0, 8)
    scores(7, 2, mx2, True)
    relay(3)
    arrive(1, 5)
    arrive(1, 6)
    send(1, 10, 11)
    loop(soft_far, 0, HQ)

    packed = jnp.zeros((64, ROWS), F32)
    for i in range(4):
        moved = stat[...] if i == 0 else pltpu.roll(stat[...], 32 * i, 1)
        packed = packed + lax.dot_general(
            table[i * 64:(i + 1) * 64], moved, (((1,), (0,)), ((), ())),
            precision=lax.Precision.HIGHEST, preferred_element_type=F32,
        )
    pack[...] = packed.reshape(8, 8, ROWS)
    stage1 = [
        pltpu.make_async_remote_copy(
            pack.at[(spot + d) % 8], t2.at[spot], s_send.at[d - 1], s_recv.at[d - 1],
            device_id=(s, plane + (spot + d) % 8), device_id_type=MESH,
        )
        for d in range(1, 8)
    ]
    for copy in stage1:
        copy.start()
    t2[pl.ds(spot, 1)] = pack[pl.ds(spot, 1)]
    pl.when(held_back)(rest.start)
    relay(4)

    for role in (7, 8):
        arrive(1, role)
    loop(weighted, 0, 16)
    for copy in stage1:
        copy.wait()
    stage2 = [
        pltpu.make_async_remote_copy(
            t2, t3.at[y], s_send.at[6 + d], s_recv.at[6 + d],
            device_id=(s, (a + 8 * d) % 32), device_id_type=MESH,
        )
        for d in range(1, 4)
    ]
    for copy in stage2:
        copy.start()
    t3[pl.ds(y, 1)] = t2[...].reshape(1, 8, 8, ROWS)
    loop(weighted, 16, HQ)
    for copy in stage2:
        copy.wait()
    turned[...] = t3[...].reshape(256, ROWS).T
    lse[0] = turned[pl.ds(pl.multiple_of(y * HQ, HQ), HQ), :]

    for t in range(2):
        for cond, copy in moves[t]:
            pl.when(cond)(copy.wait_send)
    for i in range(LONG):
        pl.when(own_long > i)(leg1(i).wait_send)
        pl.when(mid_long > i)(leg2(i).wait_send)
        pl.when((s < 7) & (own_long <= i))(piece(i).wait_send)

    @pl.when(s < 7)
    def _():
        main.wait_send()
        rest.wait_send()

    @pl.when(s > 0)
    def _():
        for i in range(LONG):
            piece(i).wait_recv()
        main.wait_recv()
        rest.wait_recv()


def deliver(*refs):
    count = len(refs) // 2
    sems = refs[-1]
    copies = [
        pltpu.make_async_copy(refs[i], refs[count + i], sems.at[i]) for i in range(count)
    ]
    for copy in copies:
        copy.start()
    for copy in copies:
        copy.wait()


def shards(queries, keys, values, handoff, doc_lengths, task_lengths, assignment):
    anywhere = pl.BlockSpec(memory_space=pltpu.HBM)
    local = pl.BlockSpec(memory_space=pltpu.VMEM)
    dma = pltpu.SemaphoreType.DMA
    results = pl.pallas_call(
        kernel,
        out_shape=(
            pltpu.VMEM((1, ROWS, HQ * HD), BF16),
            pltpu.VMEM((1, HQ, 256), F32),
            pltpu.VMEM((1, ROWS, WIDE), BF16),
        ),
        in_specs=[anywhere] * 7,
        out_specs=(local, local, local),
        scratch_shapes=[
            pltpu.VMEM((HQ, ROWS, HD), BF16),
            pltpu.VMEM((ROLES, ROWS, HK * HD), BF16),
            pltpu.VMEM((ROLES, ROWS, HK * HD), BF16),
            pltpu.VMEM((HQ, ROWS, ROLES * ROWS), F32),
            *[pltpu.VMEM((HQ, ROWS, ROWS), F32)] * 6,
            pltpu.VMEM((ROWS, ROWS), F32),
            pltpu.VMEM((256, ROWS), F32),
            pltpu.VMEM((LONG // 2 * PIECE, WIDE), BF16),
            pltpu.SMEM((1, 8), jnp.int32),
            pltpu.VMEM((32, 32), jnp.int32),
            pltpu.VMEM((32, 32), jnp.int32),
            pltpu.VMEM((8, 8, ROWS), F32),
            pltpu.VMEM((8, 8, ROWS), F32),
            pltpu.VMEM((4, 8, 8, ROWS), F32),
            pltpu.VMEM((ROWS, 256), F32),
            dma((HQ,)),
            dma((2,)),
            dma((3,)),
            dma((2, 12)),
            dma((2, ROLES)),
            dma((LONG + 2,)),
            dma((LONG + 2,)),
            dma((2 * LONG,)),
            dma((LONG,)),
            dma((10,)),
            dma((10,)),
        ],
        compiler_params=pltpu.CompilerParams(
            collective_id=0, has_side_effects=True, vmem_limit_bytes=52 << 20
        ),
    )(queries, keys, values, handoff, doc_lengths, task_lengths, assignment)
    context, stats, received = pl.pallas_call(
        deliver,
        out_shape=tuple(jax.ShapeDtypeStruct(r.shape, r.dtype) for r in results),
        in_specs=[local] * 3,
        out_specs=(anywhere,) * 3,
        scratch_shapes=[dma((3,))],
    )(*[pltpu.with_memory_space_constraint(r, pltpu.VMEM) for r in results])
    return context, jnp.swapaxes(stats, 1, 2), received


def solution(mesh):
    rows = P("section", "attn", None)
    small = P("section", None, None)
    return jax.shard_map(
        shards,
        mesh=mesh,
        in_specs=(rows, rows, rows, rows, P("section", None), small, small),
        out_specs=(rows, rows, rows),
        check_vma=False,
    )
```

time: 67.1 us -> 54.5 us (0.81)
  Pallas kernels: 63.4 us -> 53.7 us
  local copies, waits for them, and re-layouts: 2.98 us -> 0 us
    pallas_call x1, Pallas kernels: 63.4 us -> 52 us  [shards(): pl.pallas_call(kernel, out_shape=(pltpu.VMEM((1, ROWS, HQ * HD), BF16), p...]
    unnamed x2 -> x0, local copies, waits for them, and re-layouts: 2.29 us -> none
    pallas_call x0 -> x1, Pallas kernels: none -> 1.7 us  [shards(): pl.pallas_call(deliver, out_shape=tuple((jax.ShapeDtypeStruct(r.shape, r....]
    pallas_call x1 -> x0, local copies, waits for them, and re-layouts: 0.69 us -> none  [shards(): pl.pallas_call(kernel, out_shape=(pltpu.VMEM((1, ROWS, HQ * HD), BF16), p...]
where the time goes in v2:
time: 54.5 us; the launch traced here: 54.4 us
  Pallas kernels  53.7 us (99%)
  between operations  0.64 us (1%)
    pallas_call x1, Pallas kernels, shards(): pl.pallas_call(kernel, out_shape=(pltpu.VMEM((1, ROWS, HQ * HD), BF16), p...  52 us
    pallas_call x1, Pallas kernels, shards(): pl.pallas_call(deliver, out_shape=tuple((jax.ShapeDtypeStruct(r.shape, r....  1.7 us

profile of v2, /device:TPU:192, one launch (start us, length us, event | category | flops | bytes accessed | tf_op | source)
XLA Modules:
  0.0 54.4 jit_solution(9130419272611845423)
XLA Ops:
  0.6 52.0 %shard_map.94 = (bf16[1,128,4096]{2,1,0:T(8,128)(2,1)S(1)}, f32[1,32,256]{2,1,0:T(8,128)S(1)}, bf16[1,128,8192]{2,1,0:T(8,128)(2,1)S(1)}) custom-call(bf16[1,128,4096]{2,1,0:T(8,128)(2,1)} %q_hbm.1, bf16[1,128,512]{2,1,0:T(8,128)(2,1)} %k_hbm.1, bf16[1,128,512]{2,1,0:T(8,128)(2,1)} %v_hbm.1, bf16[1,128,8192]{2,1,0:T(8,128)(2,1)} %h_hbm.1, s32[1,8]{1,0:T(1,128)} %dl_hbm.1, ...), custom_call_target="tpu_custom_call" | custom-call | tf_op jit(solution)/shard_map/pallas_call | solution.py:455
  52.7 1.7 %shard_map.95 = (bf16[1,128,4096]{2,1,0:T(8,128)(2,1)}, f32[1,32,256]{2,1,0:T(8,128)}, bf16[1,128,8192]{2,1,0:T(8,128)(2,1)}) custom-call(bf16[1,128,4096]{2,1,0:T(8,128)(2,1)S(1)} %get-tuple-element.9.refs_0_, f32[1,32,256]{2,1,0:T(8,128)S(1)} %get-tuple-element.10.refs_1_, bf16[1,128,8192]{2,1,0:T(8,128)(2,1)S(1)} %get-tuple-element.11.refs_2_), custom_call_target="tpu_custom_call" | custom-call | tf_op jit(solution)/shard_map/pallas_call | solution.py:496

commit v3 on v2

--- a/solution.py
+++ b/solution.py
@@ -21,6 +21,8 @@
 PIECE = 16
 HALF = WIDE // 2
 NEAR = 7
+NEAR_HEADS = 4
+FAR_HEADS = 8
 TAIL = 16
 SCALE = HD ** -0.5
 EXP2 = SCALE / math.log(2.0)
@@ -42,9 +44,9 @@
     q_hbm, k_hbm, v_hbm, h_hbm, dl_hbm, tl_hbm, as_hbm,
     ctx, lse, rec,
     qs, kb, vb, sc, mx, mx2, top1, sum1, rl, rl2, stat, table, mid, ends, tl, ws,
-    pack, t2, t3, turned,
+    pack, t2,
     q_sem, own_sem, int_sem, kv_send, kv_recv, h_send, h_recv, m_send, m_recv,
-    s_send, s_recv,
+    s_send, s_recv, ready,
 ):
     s = lax.axis_index("section")
     a = lax.axis_index("attn")
@@ -60,12 +62,41 @@
 
     sender = (core == 1) & (z < 6)
     own_long = jnp.where(core == 1, long_pieces(z), 0)
-    mid_long = jnp.where(core == 0, long_pieces(up), 0)
+    mid_long = jnp.where(core == 1, long_pieces(up), 0)
     is_sender = own_long > 0
     is_mid = mid_long > 0
     last_long = jnp.where((core == 0) & (z >= 2), long_pieces((z + 6) % 8), 0)
     is_last = last_long > 0
 
+    barrier = pltpu.get_barrier_semaphore()
+
+    def greet(device):
+        pl.semaphore_signal(barrier, inc=1, device_id=device, device_id_type=MESH)
+
+    @pl.when(s > 0)
+    def _():
+        greet((s - 1, a))
+
+    @pl.when(is_mid)
+    def _():
+        greet((section_of(up, 1), owner_of(y, up, x)))
+
+    @pl.when(is_last)
+    def _():
+        greet((section_of(up, 1), owner_of(y, up, x)))
+
+    @pl.when((zl == 0) & (y > 0))
+    def _():
+        greet((s, a - 4))
+
+    plane = a - a % 8
+    spot = a % 8
+    for d in range(1, 8):
+        greet((s, plane + (spot + d) % 8))
+    for d in range(1, 4):
+        greet((s, (a + 8 * d) % 32))
+    expected = 10 + jnp.where(s < 7, 1, 0) + jnp.where(is_sender, 1, 0) + jnp.where(is_mid, 1, 0)
+    expected = expected + jnp.where((zl == 1) & (y < 3), 1, 0)
     for h in range(HQ):
         pltpu.make_async_copy(
             q_hbm.at[0, :, pl.ds(h * HD, HD)], qs.at[h], q_sem.at[h]
@@ -82,35 +113,6 @@
     for copy in own + ints:
         copy.start()
 
-    barrier = pltpu.get_barrier_semaphore()
-
-    def greet(device):
-        pl.semaphore_signal(barrier, inc=1, device_id=device, device_id_type=MESH)
-
-    @pl.when(s > 0)
-    def _():
-        greet((s - 1, a))
-
-    @pl.when(is_mid)
-    def _():
-        greet((section_of(up, 1), owner_of(y, up, x)))
-
-    @pl.when(is_last)
-    def _():
-        greet((section_of(up, 0), owner_of(y, up, x)))
-
-    @pl.when((zl == 0) & (y > 0))
-    def _():
-        greet((s, a - 4))
-
-    plane = a - a % 8
-    spot = a % 8
-    for d in range(1, 8):
-        greet((s, plane + (spot + d) % 8))
-    for d in range(1, 4):
-        greet((s, (a + 8 * d) % 32))
-    expected = 10 + jnp.where(s < 7, 1, 0) + jnp.where(is_sender, 1, 0) + jnp.where(is_mid, 1, 0)
-    expected = expected + jnp.where((zl == 1) & (y < 3), 1, 0)
     pl.semaphore_wait(barrier, expected)
 
     hbm = (k_hbm, v_hbm)
@@ -200,7 +202,7 @@
         rows, lanes = part(i)
         return pltpu.make_async_remote_copy(
             h_hbm.at[0, rows, lanes], mid.at[rows, lanes], m_send.at[i], m_recv.at[i],
-            device_id=(section_of(down, 0), owner_of(y, down, x)), device_id_type=MESH,
+            device_id=(section_of(down, 1), owner_of(y, down, x)), device_id_type=MESH,
         )
 
     def leg2(i):
@@ -217,11 +219,8 @@
             leg2(i).start()
 
     send(0, 1, 0, 2, 3)
-    send(1, 0, 2, 3)
-    for i in range(2):
-        pl.when(own_long > i)(leg1(i).start)
-    send(1, 1)
-    for i in range(2, LONG):
+    send(1, 1, 0, 2, 3)
+    for i in range(LONG):
         pl.when(own_long > i)(leg1(i).start)
 
     @pl.when(s < 7)
@@ -308,21 +307,35 @@
         stat[...] = jnp.where(lane == h, value, stat[...])
         return carry
 
-    def weighted(h, carry):
-        factor = jnp.concatenate(
-            [jnp.tile(rl[h], (1, NEAR)), jnp.tile(rl2[h], (1, ROLES - NEAR))], axis=1
-        )
-        weights = (sc[h] * factor).astype(BF16)
-        lanes = pl.ds(pl.multiple_of((h // GROUP) * HD, HD), HD)
-        rows = vb[:, :, lanes].reshape(ROLES * ROWS, HD)
-        out = lax.dot_general(
-            weights, rows, (((1,), (0,)), ((), ())), preferred_element_type=F32
-        )
-        ctx[0, :, pl.ds(pl.multiple_of(h * HD, HD), HD)] = out.astype(BF16)
+    def weighted(step, heads, low, high, factor):
+        chosen = pl.ds(step * heads, heads)
+        lift = jnp.tile(factor[chosen], (1, 1, high - low))
+        weights = (sc[chosen, :, low * ROWS:high * ROWS] * lift).astype(BF16)
+        lanes = pl.ds(pl.multiple_of((step * heads // GROUP) * HD, HD), HD)
+        rows = vb[low:high, :, lanes].reshape((high - low) * ROWS, HD)
+        return lax.dot_general(
+            weights.reshape(heads * ROWS, (high - low) * ROWS), rows,
+            (((1,), (0,)), ((), ())), preferred_element_type=F32,
+        ).reshape(heads, ROWS, HD)
+
+    def weighted_near(step, carry):
+        top1[pl.ds(step * NEAR_HEADS, NEAR_HEADS)] = weighted(step, NEAR_HEADS, 0, NEAR, rl)
         return carry
 
+    def weighted_far(step, carry):
+        out = weighted(step, FAR_HEADS, NEAR, ROLES, rl2)
+        out = (out + top1[pl.ds(step * FAR_HEADS, FAR_HEADS)]).astype(BF16)
+        for i in range(FAR_HEADS):
+            ctx[0, :, pl.ds(pl.multiple_of((step * FAR_HEADS + i) * HD, HD), HD)] = out[i]
+        return carry
+
     def loop(body, low, high):
-        lax.fori_loop(low, high, body, 0, unroll=2)
+        lax.fori_loop(low, high, body, 0, unroll=4)
+
+    for d in range(1, 4):
+        pl.semaphore_signal(
+            ready, inc=1, device_id=(s, (a + 8 * d) % 32), device_id_type=MESH
+        )
 
     scores(0, 1, mx, True)
     arrive(0, 1)
@@ -331,14 +344,15 @@
     send(0, 6, 7)
 
     slots = lax.broadcasted_iota(jnp.int32, (256, 32), 0)
+    slot_rank = slots // 64 + 4 * (slots % 2)
     tasks = lax.broadcasted_iota(jnp.int32, (256, 32), 1)
     lengths = tl[pl.ds(a, 1), :]
     workers = ws[pl.ds(a, 1), :]
-    picked = workers == slots // 8
+    picked = workers == slots % 64 // 2
     which = jnp.sum(jnp.where(picked, tasks, 0), axis=1, keepdims=True)
     length = jnp.sum(jnp.where(picked, lengths, 0), axis=1, keepdims=True)
     start = jnp.sum(jnp.where(tasks < which, lengths, 0), axis=1, keepdims=True)
-    rank = lax.broadcasted_iota(jnp.int32, (256, ROWS), 0) % 8
+    rank = slot_rank[:, :1]
     token = lax.broadcasted_iota(jnp.int32, (256, ROWS), 1)
     table[...] = jnp.where((token == start + rank) & (rank < length), F32(1), F32(0))
     stat[...] = jnp.zeros_like(stat)
@@ -373,6 +387,7 @@
     send(1, 10, 11)
     loop(soft_far, 0, HQ)
 
+    pl.semaphore_wait(ready, 3)
     packed = jnp.zeros((64, ROWS), F32)
     for i in range(4):
         moved = stat[...] if i == 0 else pltpu.roll(stat[...], 32 * i, 1)
@@ -380,40 +395,35 @@
             table[i * 64:(i + 1) * 64], moved, (((1,), (0,)), ((), ())),
             precision=lax.Precision.HIGHEST, preferred_element_type=F32,
         )
-    pack[...] = packed.reshape(8, 8, ROWS)
-    stage1 = [
+    pack[...] = packed.reshape(32, 2, ROWS)
+    tasks_out = [
         pltpu.make_async_remote_copy(
-            pack.at[(spot + d) % 8], t2.at[spot], s_send.at[d - 1], s_recv.at[d - 1],
-            device_id=(s, plane + (spot + d) % 8), device_id_type=MESH,
-        )
-        for d in range(1, 8)
+            pack.at[(a + d) % 32], t2.at[a], s_send.at[d - 1], s_recv.at[d - 1],
+            device_id=(s, (a + d) % 32), device_id_type=MESH,
+        )
+        for d in range(1, 32)
     ]
-    for copy in stage1:
+    for copy in tasks_out:
         copy.start()
-    t2[pl.ds(spot, 1)] = pack[pl.ds(spot, 1)]
+    t2[pl.ds(a, 1)] = pack[pl.ds(a, 1)]
     pl.when(held_back)(rest.start)
     relay(4)
 
+    lax.fori_loop(0, HQ // NEAR_HEADS, weighted_near, 0)
     for role in (7, 8):
         arrive(1, role)
-    loop(weighted, 0, 16)
-    for copy in stage1:
+    lax.fori_loop(0, HQ // FAR_HEADS, weighted_far, 0)
+    for copy in tasks_out:
         copy.wait()
-    stage2 = [
-        pltpu.make_async_remote_copy(
-            t2, t3.at[y], s_send.at[6 + d], s_recv.at[6 + d],
-            device_id=(s, (a + 8 * d) % 32), device_id_type=MESH,
-        )
-        for d in range(1, 4)
-    ]
-    for copy in stage2:
-        copy.start()
-    t3[pl.ds(y, 1)] = t2[...].reshape(1, 8, 8, ROWS)
-    loop(weighted, 16, HQ)
-    for copy in stage2:
-        copy.wait()
-    turned[...] = t3[...].reshape(256, ROWS).T
-    lse[0] = turned[pl.ds(pl.multiple_of(y * HQ, HQ), HQ), :]
+    turned = t2[...].reshape(64, ROWS).T
+    turned = jnp.concatenate([turned[32 * i:32 * (i + 1)] for i in range(4)], axis=1)
+    source = lax.broadcasted_iota(jnp.int32, (256, 256), 0)
+    slot = lax.broadcasted_iota(jnp.int32, (256, 256), 1)
+    spread = jnp.where(slot == 4 * (source % 64) + source // 64, F32(1), F32(0))
+    lse[0] = lax.dot_general(
+        turned, spread, (((1,), (0,)), ((), ())),
+        precision=lax.Precision.HIGHEST, preferred_element_type=F32,
+    )
 
     for t in range(2):
         for cond, copy in moves[t]:
@@ -473,10 +483,8 @@
             pltpu.SMEM((1, 8), jnp.int32),
             pltpu.VMEM((32, 32), jnp.int32),
             pltpu.VMEM((32, 32), jnp.int32),
-            pltpu.VMEM((8, 8, ROWS), F32),
-            pltpu.VMEM((8, 8, ROWS), F32),
-            pltpu.VMEM((4, 8, 8, ROWS), F32),
-            pltpu.VMEM((ROWS, 256), F32),
+            pltpu.VMEM((32, 2, ROWS), F32),
+            pltpu.VMEM((32, 2, ROWS), F32),
             dma((HQ,)),
             dma((2,)),
             dma((3,)),
@@ -486,8 +494,9 @@
             dma((LONG + 2,)),
             dma((2 * LONG,)),
             dma((LONG,)),
-            dma((10,)),
-            dma((10,)),
+            dma((31,)),
+            dma((31,)),
+            pltpu.SemaphoreType.REGULAR,
         ],
         compiler_params=pltpu.CompilerParams(
             collective_id=0, has_side_effects=True, vmem_limit_bytes=52 << 20

time: 54.5 us -> 51 us (0.936)
  Pallas kernels: 53.7 us -> 50.3 us
    pallas_call x1, Pallas kernels: 52 us -> 48.6 us  [shards(): pl.pallas_call(kernel, out_shape=(pltpu.VMEM((1, ROWS, HQ * HD), BF16), p...]
where the time goes in v3:
time: 51 us; the launch traced here: 50.9 us
  Pallas kernels  50.3 us (99%)
  between operations  0.64 us (1%)
    pallas_call x1, Pallas kernels, shards(): pl.pallas_call(kernel, out_shape=(pltpu.VMEM((1, ROWS, HQ * HD), BF16), p...  48.6 us
    pallas_call x1, Pallas kernels, shards(): pl.pallas_call(deliver, out_shape=tuple((jax.ShapeDtypeStruct(r.shape, r....  1.7 us

profile of v3, /device:TPU:192, one launch (start us, length us, event | category | flops | bytes accessed | tf_op | source)
XLA Modules:
  0.0 50.9 jit_solution(7097391335405106431)
XLA Ops:
  0.6 48.6 %shard_map.94 = (bf16[1,128,4096]{2,1,0:T(8,128)(2,1)S(1)}, f32[1,32,256]{2,1,0:T(8,128)S(1)}, bf16[1,128,8192]{2,1,0:T(8,128)(2,1)S(1)}) custom-call(bf16[1,128,4096]{2,1,0:T(8,128)(2,1)} %q_hbm.1, bf16[1,128,512]{2,1,0:T(8,128)(2,1)} %k_hbm.1, bf16[1,128,512]{2,1,0:T(8,128)(2,1)} %v_hbm.1, bf16[1,128,8192]{2,1,0:T(8,128)(2,1)} %h_hbm.1, s32[1,8]{1,0:T(1,128)} %dl_hbm.1, ...), custom_call_target="tpu_custom_call" | custom-call | tf_op jit(solution)/shard_map/pallas_call | solution.py:465
  49.2 1.7 %shard_map.95 = (bf16[1,128,4096]{2,1,0:T(8,128)(2,1)}, f32[1,32,256]{2,1,0:T(8,128)}, bf16[1,128,8192]{2,1,0:T(8,128)(2,1)}) custom-call(bf16[1,128,4096]{2,1,0:T(8,128)(2,1)S(1)} %get-tuple-element.9.refs_0_, f32[1,32,256]{2,1,0:T(8,128)S(1)} %get-tuple-element.10.refs_1_, bf16[1,128,8192]{2,1,0:T(8,128)(2,1)S(1)} %get-tuple-element.11.refs_2_), custom_call_target="tpu_custom_call" | custom-call | tf_op jit(solution)/shard_map/pallas_call | solution.py:505

commit v4 on v3

--- a/solution.py
+++ b/solution.py
@@ -46,7 +46,7 @@
     qs, kb, vb, sc, mx, mx2, top1, sum1, rl, rl2, stat, table, mid, ends, tl, ws,
     pack, t2,
     q_sem, own_sem, int_sem, kv_send, kv_recv, h_send, h_recv, m_send, m_recv,
-    s_send, s_recv, ready,
+    s_send, s_recv, ready, met,
 ):
     s = lax.axis_index("section")
     a = lax.axis_index("attn")
@@ -91,11 +91,13 @@
 
     plane = a - a % 8
     spot = a % 8
-    for d in range(1, 8):
-        greet((s, plane + (spot + d) % 8))
+    partner = plane + (spot + 4) % 8
+    greet((s, partner))
+    for d in range(1, 4):
+        greet((s, a - x + (x + d) % 4))
     for d in range(1, 4):
         greet((s, (a + 8 * d) % 32))
-    expected = 10 + jnp.where(s < 7, 1, 0) + jnp.where(is_sender, 1, 0) + jnp.where(is_mid, 1, 0)
+    expected = 7 + jnp.where(s < 7, 1, 0) + jnp.where(is_sender, 1, 0) + jnp.where(is_mid, 1, 0)
     expected = expected + jnp.where((zl == 1) & (y < 3), 1, 0)
     for h in range(HQ):
         pltpu.make_async_copy(
@@ -115,6 +117,8 @@
 
     pl.semaphore_wait(barrier, expected)
 
+    pl.semaphore_signal(met, inc=1, device_id=(s, partner), device_id_type=MESH)
+
     hbm = (k_hbm, v_hbm)
     buf = (kb, vb)
 
@@ -332,6 +336,7 @@
     def loop(body, low, high):
         lax.fori_loop(low, high, body, 0, unroll=4)
 
+    pl.semaphore_wait(met, 1)
     for d in range(1, 4):
         pl.semaphore_signal(
             ready, inc=1, device_id=(s, (a + 8 * d) % 32), device_id_type=MESH
@@ -497,6 +502,7 @@
             dma((31,)),
             dma((31,)),
             pltpu.SemaphoreType.REGULAR,
+            pltpu.SemaphoreType.REGULAR,
         ],
         compiler_params=pltpu.CompilerParams(
             collective_id=0, has_side_effects=True, vmem_limit_bytes=52 << 20

time: 51 us -> 50.1 us (0.982)
  Pallas kernels: 50.3 us -> 49.3 us
    pallas_call x1, Pallas kernels: 48.6 us -> 47.6 us  [shards(): pl.pallas_call(kernel, out_shape=(pltpu.VMEM((1, ROWS, HQ * HD), BF16), p...]
where the time goes in v4:
time: 50.1 us; the launch traced here: 50 us
  Pallas kernels  49.3 us (98%)
  between operations  0.64 us (1%)
    pallas_call x1, Pallas kernels, shards(): pl.pallas_call(kernel, out_shape=(pltpu.VMEM((1, ROWS, HQ * HD), BF16), p...  47.6 us
    pallas_call x1, Pallas kernels, shards(): pl.pallas_call(deliver, out_shape=tuple((jax.ShapeDtypeStruct(r.shape, r....  1.7 us

profile of v4, /device:TPU:192, one launch (start us, length us, event | category | flops | bytes accessed | tf_op | source)
XLA Modules:
  0.0 50.0 jit_solution(14811865256329974416)
XLA Ops:
  0.6 47.6 %shard_map.94 = (bf16[1,128,4096]{2,1,0:T(8,128)(2,1)S(1)}, f32[1,32,256]{2,1,0:T(8,128)S(1)}, bf16[1,128,8192]{2,1,0:T(8,128)(2,1)S(1)}) custom-call(bf16[1,128,4096]{2,1,0:T(8,128)(2,1)} %q_hbm.1, bf16[1,128,512]{2,1,0:T(8,128)(2,1)} %k_hbm.1, bf16[1,128,512]{2,1,0:T(8,128)(2,1)} %v_hbm.1, bf16[1,128,8192]{2,1,0:T(8,128)(2,1)} %h_hbm.1, s32[1,8]{1,0:T(1,128)} %dl_hbm.1, ...), custom_call_target="tpu_custom_call" | custom-call | tf_op jit(solution)/shard_map/pallas_call | solution.py:470
  48.3 1.7 %shard_map.95 = (bf16[1,128,4096]{2,1,0:T(8,128)(2,1)}, f32[1,32,256]{2,1,0:T(8,128)}, bf16[1,128,8192]{2,1,0:T(8,128)(2,1)}) custom-call(bf16[1,128,4096]{2,1,0:T(8,128)(2,1)S(1)} %get-tuple-element.9.refs_0_, f32[1,32,256]{2,1,0:T(8,128)S(1)} %get-tuple-element.10.refs_1_, bf16[1,128,8192]{2,1,0:T(8,128)(2,1)S(1)} %get-tuple-element.11.refs_2_), custom_call_target="tpu_custom_call" | custom-call | tf_op jit(solution)/shard_map/pallas_call | solution.py:511
